TPU v7x, 256 devices: a whole 4x4x8 slice. The times are simulated.
256 devices in a mesh: dp: 8 (over z_lo, core), seq: 32 (over y, x, z_hi).
Axes of the slice: x: 4, y: 4, z: 8 (z_hi: 2, z_lo: 4; z = z_hi * 4 + z_lo), core: 2. Of those that a mesh axis runs over, the one named last changes fastest.
Arguments:
- first_input: bfloat16 [8, 16384, 128], P('dp', 'seq'), may hold values from -6 to 6
- value_input: bfloat16 [8, 16384, 128], P('dp', 'seq'), may hold values from -6 to 6
- gate_input: bfloat16 [8, 16384, 128], P('dp', 'seq'), may hold values from -6 to 6
- cotangent: bfloat16 [8, 16384, 128], P('dp', 'seq'), may hold values from -6 to 6
- filter_taps: float32 [16384, 128], P('seq'), may hold values from -4 to 4
- skip_weight: float32 [128], replicated, may hold values from -4 to 4
Outputs:
- layer_output: bfloat16 [8, 16384, 128], P('dp', 'seq')
- filter_grad: float32 [16384, 128], P('seq')
All inputs are finite; a program needn't handle non-finite values.
Results may differ from a plain program's by a relative error of at most 0.001.
Values sent between devices are 32-bit elements; how exact they have to be, the bound alone decides.
A program may use at most 64 MiB of HBM per device.

v0:
```python
import functools
import math
import jax
import jax.numpy as jnp
from jax import lax
from jax.sharding import PartitionSpec as P


def angles(numer, period):
    return 2.0 * math.pi / period * (numer % period).astype(jnp.float32)


def rotate(real_part, imag_part, phase, direction):
    cosine = jnp.cos(phase)
    sine = direction * jnp.sin(phase)
    return (real_part * cosine - imag_part * sine, real_part * sine + imag_part * cosine)


def local_transform(real_part, imag_part, direction):
    count, length = real_part.shape
    outer = 1 << (length.bit_length() - 1) // 2
    inner = length // outer
    real_cube = real_part.reshape(count, outer, inner)
    imag_cube = imag_part.reshape(count, outer, inner)
    outer_idx = lax.iota(jnp.int32, outer)
    inner_idx = lax.iota(jnp.int32, inner)
    first_phase = angles(outer_idx[:, None] * outer_idx[None, :], outer)
    first_cos = jnp.cos(first_phase)
    first_sin = direction * jnp.sin(first_phase)
    mix = functools.partial(
        jnp.einsum, precision=lax.Precision.HIGHEST, preferred_element_type=jnp.float32
    )
    section_real = mix("kp,cpq->ckq", first_cos, real_cube) - mix(
        "kp,cpq->ckq", first_sin, imag_cube
    )
    section_imag = mix("kp,cpq->ckq", first_cos, imag_cube) + mix(
        "kp,cpq->ckq", first_sin, real_cube
    )
    twiddle = angles(outer_idx[:, None] * inner_idx[None, :], length)
    section_real, section_imag = rotate(section_real, section_imag, twiddle, direction)
    second_phase = angles(inner_idx[:, None] * inner_idx[None, :], inner)
    second_cos = jnp.cos(second_phase)
    second_sin = direction * jnp.sin(second_phase)
    final_real = mix("ckq,jq->ckj", section_real, second_cos) - mix(
        "ckq,jq->ckj", section_imag, second_sin
    )
    final_imag = mix("ckq,jq->ckj", section_imag, second_cos) + mix(
        "ckq,jq->ckj", section_real, second_sin
    )
    final_real = jnp.transpose(final_real, (0, 2, 1)).reshape(count, length)
    final_imag = jnp.transpose(final_imag, (0, 2, 1)).reshape(count, length)
    return (final_real, final_imag)


def channel_layout(gated, weighted, filter_taps, gate_input, skip_weight):
    batch_local = gated.shape[0]
    moved_gated, moved_weighted, moved_taps = (
        lax.all_to_all(gated, "seq", split_axis=2, concat_axis=1, tiled=True),
        lax.all_to_all(weighted, "seq", split_axis=2, concat_axis=1, tiled=True),
        lax.all_to_all(filter_taps[None], "seq", split_axis=2, concat_axis=1, tiled=True),
    )
    length = moved_gated.shape[1]
    narrow = moved_gated.shape[2]
    spread = batch_local * narrow
    gated_rows = jnp.transpose(moved_gated, (0, 2, 1)).reshape(spread, length)
    weighted_rows = jnp.transpose(moved_weighted, (0, 2, 1)).reshape(spread, length)
    taps_rows = jnp.transpose(moved_taps[0], (1, 0))
    rows_all = jnp.concatenate([gated_rows, taps_rows, weighted_rows], axis=0)
    count = rows_all.shape[0]
    twist = angles(lax.iota(jnp.int32, length), 2 * length)[None, :]
    cos_twist = jnp.cos(twist)
    sin_twist = jnp.sin(twist)
    real_in = jnp.concatenate([rows_all, rows_all * cos_twist], axis=0)
    imag_in = jnp.concatenate([jnp.zeros_like(rows_all), -rows_all * sin_twist], axis=0)
    spec_real, spec_imag = local_transform(real_in, imag_in, -1.0)
    spec_real = spec_real.reshape(2, count, length)
    spec_imag = spec_imag.reshape(2, count, length)
    gated_real = spec_real[:, :spread].reshape(2, batch_local, narrow, length)
    gated_imag = spec_imag[:, :spread].reshape(2, batch_local, narrow, length)
    taps_real = spec_real[:, spread : spread + narrow][:, None]
    taps_imag = spec_imag[:, spread : spread + narrow][:, None]
    source_real = spec_real[:, spread + narrow :].reshape(2, batch_local, narrow, length)
    source_imag = spec_imag[:, spread + narrow :].reshape(2, batch_local, narrow, length)
    conv_real = (gated_real * taps_real - gated_imag * taps_imag).reshape(2, spread, length)
    conv_imag = (gated_real * taps_imag + gated_imag * taps_real).reshape(2, spread, length)
    grad_real = jnp.sum(source_real * gated_real + source_imag * gated_imag, axis=1)
    grad_imag = jnp.sum(source_imag * gated_real - source_real * gated_imag, axis=1)
    back_real = jnp.concatenate([conv_real, grad_real], axis=1).reshape(-1, length)
    back_imag = jnp.concatenate([conv_imag, grad_imag], axis=1).reshape(-1, length)
    back_real, back_imag = local_transform(back_real, back_imag, 1.0)
    back_real = back_real.reshape(2, -1, length)
    back_imag = back_imag.reshape(2, -1, length)
    joined = (back_real[0] + back_real[1] * cos_twist - back_imag[1] * sin_twist) / (2.0 * length)
    convolved = jnp.transpose(joined[:spread].reshape(batch_local, narrow, length), (0, 2, 1))
    grad_time = lax.psum(jnp.transpose(joined[spread:], (1, 0)), "dp")
    convolved, grad_back = (
        lax.all_to_all(convolved, "seq", split_axis=1, concat_axis=2, tiled=True),
        lax.all_to_all(grad_time[None], "seq", split_axis=1, concat_axis=2, tiled=True),
    )
    layer_output = (gate_input.astype(jnp.float32) * (convolved + skip_weight * gated)).astype(
        jnp.bfloat16
    )
    scale = 1.0 / math.sqrt(batch_local * lax.axis_size("dp") * length)
    return (layer_output, grad_back[0] * scale)


def shards(first_input, value_input, gate_input, cotangent, filter_taps, skip_weight):
    gated = first_input.astype(jnp.float32) * value_input.astype(jnp.float32)
    weighted = cotangent.astype(jnp.float32) * gate_input.astype(jnp.float32)
    return channel_layout(gated, weighted, filter_taps, gate_input, skip_weight)


def solution(mesh):
    placed = (
        P("dp", "seq", None),
        P("dp", "seq", None),
        P("dp", "seq", None),
        P("dp", "seq", None),
        P("seq", None),
        P(),
    )
    return jax.shard_map(
        shards,
        mesh=mesh,
        in_specs=placed,
        out_specs=(P("dp", "seq", None), P("seq", None)),
        check_vma=False,
    )
```

profile of v0, /device:TPU:2, one launch (start us, length us, event | category | flops | bytes accessed | tf_op | source)
XLA Modules:
  0.0 486.5 jit_solution(10669566144408117033)
XLA Ops:
  7.2 1.1 convert_multiply_fusion.1
  8.3 0.8 copy.157
  9.1 14.2 %all-to-all-start.2 = ((f32[1,512,128]{1,0,2:T(1,128)}), f32[1,512,128]{1,0,2:T(1,128)S(1)}, u32[]{:S(2)}, u32[]{:S(2)}) async-start(f32[1,512,128]{1,0,2:T(1,128)} %copy.157), calls=%async_computation.2 | async-start | bytes 524288 | tf_op jit(solution)/shard_map/all_to_all | solution.py:59
  23.4 0.8 copy.211
  24.2 11.4 %all-to-all-done.2 = f32[1,512,128]{1,0,2:T(1,128)S(1)} async-done(((f32[1,512,128]{1,0,2:T(1,128)}), f32[1,512,128]{1,0,2:T(1,128)S(1)}, u32[]{:S(2)}, u32[]{:S(2)}) %all-to-all-start.2) | async-done | bytes 262176 | tf_op jit(solution)/shard_map/all_to_all | solution.py:59
  35.6 5.0 %all-to-all-start.1 = ((f32[1,512,128]{1,0,2:T(1,128)}), f32[1,512,128]{1,0,2:T(1,128)S(1)}, u32[]{:S(2)}, u32[]{:S(2)}) async-start(f32[1,512,128]{1,0,2:T(1,128)} %copy.211), calls=%async_computation.1 | async-start | bytes 524288 | tf_op jit(solution)/shard_map/all_to_all | solution.py:60
  40.6 0.8 copy.153
  41.4 0.3 fusion.72
  41.7 0.3 fusion.71
  42.0 0.3 broadcast_multiply_fusion.1
  42.2 10.6 %all-to-all-done.1 = f32[1,512,128]{1,0,2:T(1,128)S(1)} async-done(((f32[1,512,128]{1,0,2:T(1,128)}), f32[1,512,128]{1,0,2:T(1,128)S(1)}, u32[]{:S(2)}, u32[]{:S(2)}) %all-to-all-start.1) | async-done | bytes 262176 | tf_op jit(solution)/shard_map/all_to_all | solution.py:60
  52.9 6.1 %all-to-all-start = ((f32[1,512,128]{1,0,2:T(1,128)}), f32[1,512,128]{1,0,2:T(1,128)S(1)}, u32[]{:S(2)}, u32[]{:S(2)}) async-start(f32[1,512,128]{1,0,2:T(1,128)} %copy.153), calls=%async_computation | async-start | bytes 524288 | tf_op jit(solution)/shard_map/all_to_all | solution.py:58
  59.0 0.2 fusion.22
  59.4 0.7 copy.181
  60.5 0.9 fusion.50
  62.3 8.7 %all-to-all-done = f32[1,512,128]{1,0,2:T(1,128)S(1)} async-done(((f32[1,512,128]{1,0,2:T(1,128)}), f32[1,512,128]{1,0,2:T(1,128)S(1)}, u32[]{:S(2)}, u32[]{:S(2)}) %all-to-all-start) | async-done | bytes 262176 | tf_op jit(solution)/shard_map/all_to_all | solution.py:58
  71.8 0.3 copy.217
  72.1 1.7 fusion.7
  73.8 2.8 fusion.45
  76.6 2.8 convolution_subtract_fusion
  79.5 1.7 convolution_add_fusion
  81.1 3.4 fusion.11
  84.5 4.0 fusion.15
  88.5 4.0 add_bitcast_fusion
  92.5 3.0 copy.175
  95.6 3.1 reshape_reshape.15
  98.6 5.4 %subtract_bitcast_fusion = f32[24,128,128]{1,2,0:T(8,128)} fusion(f32[24,128,128]{2,1,0:T(8,128)} %fusion.15, f32[24,128,128]{2,1,0:T(8,128)S(1)} %convolution_add_fusion, f32[24,128,128]{2,1,0:T(8,128)S(1)} %convolution_subtract_fusion, f32[128,128]{0,1:T(8,128)S(1)} %copy.169, f32[128,128]{0,1:T(8,128)S(1)} %copy.167), kind=kOutput, calls=%fused_computation.8 | convolution fusion | flops 605798400 | bytes 6422528 | tf_op jit(solution)/shard_map/ckq,jq->ckj/dot_general | solution.py:44
  104.0 3.2 copy.172
  107.2 3.2 reshape_reshape.14
  110.4 2.4 multiply_subtract_fusion.2
  112.8 0.4 maximum_bitcast_fusion
  113.5 1.9 fusion.41
  115.7 1.9 fusion.39
  117.6 1.9 fusion.5
  119.5 1.9 fusion.4
  121.5 2.0 fusion.18
  123.5 2.2 fusion.17
  125.7 2.0 fusion.2
  127.7 0.8 slice.55
  128.5 2.0 copy.188
  130.6 2.0 fusion.3
  133.1 0.6 copy-done.5
  133.7 0.9 fusion.9
  134.7 0.8 slice_bitcast_fusion
  135.5 12.0 %copy.189 = f32[1,16384,4]{2,0,1:T(1,128)} copy(f32[1,16384,4]{1,2,0:T(4,128)S(1)} %get-tuple-element.17) | data formatting | bytes 524288 | tf_op jit(solution)/shard_map/transpose | solution.py:94
  147.5 0.6 broadcast.236
  148.0 74.5 %reduce = f32[16384,4]{1,0:T(8,128)} reduce(f32[16384,1,4]{2,1,0:T(1,128)} %bitcast.179, f32[]{:T(128)} %broadcast.236), dimensions={1}, to_apply=%bitcast.163.reduce_sub_computation | reduce | bytes 524292
  222.6 9.5 %reshape.143 = f32[32,1,2048]{2,1,0:T(1,128)} reshape(f32[16384,4]{1,0:T(8,128)} %reduce) | data formatting | bytes 524288
  232.0 5.9 %all-to-all-start.3 = ((f32[32,1,2048]{2,1,0:T(1,128)}), f32[32,1,2048]{2,1,0:T(1,128)S(1)}, u32[]{:S(2)}, u32[]{:S(2)}) async-start(f32[32,1,2048]{2,1,0:T(1,128)} %reshape.143), calls=%async_computation.3 | async-start | bytes 524288 | tf_op jit(solution)/shard_map/all_to_all | solution.py:97
  238.0 0.7 all-reduce.3.cloned.1.call-update
  238.7 77.0 %all-reduce.3.cloned.1.call-done = f32[1,16384,4]{1,2,0:T(4,128)} async-done(((f32[1,16384,4]{1,2,0:T(4,128)}), f32[1,16384,4]{1,2,0:T(4,128)}) %all-reduce.3.cloned.1.call-update) | async-done | bytes 262160 | tf_op jit(solution)/shard_map/psum | solution.py:95
  315.7 14.8 %copy.193 = f32[1,16384,4]{2,0,1:T(1,128)} copy(f32[1,16384,4]{1,2,0:T(4,128)} %all-reduce.3.cloned.1.call-done) | data formatting | bytes 524288 | tf_op jit(solution)/shard_map/psum | solution.py:95
  330.6 74.5 %reduce.2 = f32[16384,4]{1,0:T(8,128)} reduce(f32[16384,1,4]{2,1,0:T(1,128)} %bitcast.180, f32[]{:T(128)} %broadcast.236), dimensions={1}, to_apply=%bitcast.165.reduce_sub_computation | reduce | bytes 524292
  405.1 9.1 %reshape.145 = f32[32,1,2048]{2,1,0:T(1,128)} reshape(f32[16384,4]{1,0:T(8,128)} %reduce.2) | data formatting | bytes 524288
  414.2 10.4 %all-to-all-start.4 = ((f32[32,1,2048]{2,1,0:T(1,128)}), f32[32,1,2048]{2,1,0:T(1,128)S(1)}, u32[]{:S(2)}, u32[]{:S(2)}) async-start(f32[32,1,2048]{2,1,0:T(1,128)} %reshape.145), calls=%async_computation.4 | async-start | bytes 524288 | tf_op jit(solution)/shard_map/all_to_all | solution.py:98
  424.6 1.3 reduce.1
  425.9 14.8 %reshape.144 = f32[16384,1,4]{2,1,0:T(1,128)} reshape(f32[32,2048]{1,0:T(8,128)S(1)} %reduce.1) | data formatting | bytes 524288
  440.6 5.3 %copy.212 = f32[1,32,512,4]{2,1,3,0:T(8,128)S(1)} copy(f32[1,32,512,4]{3,2,1,0:T(8,128)} %bitcast.181) | data formatting | bytes 524288 | tf_op jit(solution)/shard_map/all_to_all | solution.py:97
  445.9 0.3 copy.191
  446.4 0.7 fusion.19
  447.1 1.3 reduce.3
  448.4 14.8 %reshape.146 = f32[16384,1,4]{2,1,0:T(1,128)} reshape(f32[32,2048]{1,0:T(8,128)S(1)} %reduce.3) | data formatting | bytes 524288
  463.2 15.0 %copy.194 = f32[1,16384,4]{1,2,0:T(4,128)S(1)} copy(f32[1,16384,4]{2,0,1:T(1,128)} %bitcast.182) | data formatting | bytes 524288 | tf_op jit(solution)/shard_map/all_to_all | solution.py:98
  478.6 0.8 copy.196
  (66 shorter events, 3.7 us)
Async XLA Ops:
  7.2 16.2 %copy-start.15 = (f32[512,128]{1,0:T(8,128)S(1)}, f32[512,128]{1,0:T(8,128)}, u32[]{:S(2)}) copy-start(f32[512,128]{1,0:T(8,128)} %param.10) | copy-start | bytes 786436
  7.2 33.4 %copy-start.10 = (bf16[1,512,128]{2,1,0:T(8,128)(2,1)S(1)}, bf16[1,512,128]{2,1,0:T(8,128)(2,1)}, u32[]{:S(2)}) copy-start(bf16[1,512,128]{2,1,0:T(8,128)(2,1)} %param.7) | copy-start | bytes 393220
  7.2 33.4 %copy-start.12 = (bf16[1,512,128]{2,1,0:T(8,128)(2,1)S(1)}, bf16[1,512,128]{2,1,0:T(8,128)(2,1)}, u32[]{:S(2)}) copy-start(bf16[1,512,128]{2,1,0:T(8,128)(2,1)} %param.6) | copy-start | bytes 393220
  9.1 26.5 %all-to-all-start.2 = ((f32[1,512,128]{1,0,2:T(1,128)}), f32[1,512,128]{1,0,2:T(1,128)S(1)}, u32[]{:S(2)}, u32[]{:S(2)}) async-start(f32[1,512,128]{1,0,2:T(1,128)} %copy.157), calls=%async_computation.2 | async-start | bytes 524288 | tf_op jit(solution)/shard_map/all_to_all | solution.py:59
  35.6 17.3 %all-to-all-start.1 = ((f32[1,512,128]{1,0,2:T(1,128)}), f32[1,512,128]{1,0,2:T(1,128)S(1)}, u32[]{:S(2)}, u32[]{:S(2)}) async-start(f32[1,512,128]{1,0,2:T(1,128)} %copy.211), calls=%async_computation.1 | async-start | bytes 524288 | tf_op jit(solution)/shard_map/all_to_all | solution.py:60
  52.9 18.1 %all-to-all-start = ((f32[1,512,128]{1,0,2:T(1,128)}), f32[1,512,128]{1,0,2:T(1,128)S(1)}, u32[]{:S(2)}, u32[]{:S(2)}) async-start(f32[1,512,128]{1,0,2:T(1,128)} %copy.153), calls=%async_computation | async-start | bytes 524288 | tf_op jit(solution)/shard_map/all_to_all | solution.py:58
  60.5 10.9 %copy-start.7 = (f32[16384]{0:T(1024)}, f32[16384]{0:T(1024)S(1)}, u32[]{:S(2)}) copy-start(f32[16384]{0:T(1024)S(1)} %fusion.51) | copy-start | bytes 196612
  62.3 9.8 %copy-start.1 = (f32[4,128,128]{1,2,0:T(8,128)}, f32[4,128,128]{1,2,0:T(8,128)S(1)}, u32[]{:S(2)}) copy-start(f32[4,128,128]{1,2,0:T(8,128)S(1)} %copy.164) | copy-start | bytes 786436
  71.4 0.7 copy-start.3
  76.6 2.9 copy-start.2
  76.6 2.9 copy-start.4
  107.2 3.2 copy-start
  119.5 1.9 copy-start.6
  132.7 1.0 copy-start.5
  132.7 1.0 copy-start.8
  132.7 1.0 copy-start.14
  232.0 182.2 %all-to-all-start.3 = ((f32[32,1,2048]{2,1,0:T(1,128)}), f32[32,1,2048]{2,1,0:T(1,128)S(1)}, u32[]{:S(2)}, u32[]{:S(2)}) async-start(f32[32,1,2048]{2,1,0:T(1,128)} %reshape.143), calls=%async_computation.3 | async-start | bytes 524288 | tf_op jit(solution)/shard_map/all_to_all | solution.py:97
  238.0 77.8 %all-reduce.3.cloned.1.call-start = ((), (), s32[]{:S(2)}) async-start(), calls=%async_computation.5 | async-start | bytes 524288 | tf_op jit(solution)/shard_map/psum | solution.py:95
  414.2 33.0 %all-to-all-start.4 = ((f32[32,1,2048]{2,1,0:T(1,128)}), f32[32,1,2048]{2,1,0:T(1,128)S(1)}, u32[]{:S(2)}, u32[]{:S(2)}) async-start(f32[32,1,2048]{2,1,0:T(1,128)} %reshape.145), calls=%async_computation.4 | async-start | bytes 524288 | tf_op jit(solution)/shard_map/all_to_all | solution.py:98
  440.6 5.7 %copy-start.9 = (bf16[1,512,128]{2,1,0:T(8,128)(2,1)S(1)}, bf16[1,512,128]{2,1,0:T(8,128)(2,1)}, u32[]{:S(2)}) copy-start(bf16[1,512,128]{2,1,0:T(8,128)(2,1)} %param.8) | copy-start | bytes 393220
  440.6 5.7 %copy-start.11 = (bf16[1,512,128]{2,1,0:T(8,128)(2,1)S(1)}, bf16[1,512,128]{2,1,0:T(8,128)(2,1)}, u32[]{:S(2)}) copy-start(bf16[1,512,128]{2,1,0:T(8,128)(2,1)} %param.7) | copy-start | bytes 393220
  440.6 5.7 %copy-start.13 = (bf16[1,512,128]{2,1,0:T(8,128)(2,1)S(1)}, bf16[1,512,128]{2,1,0:T(8,128)(2,1)}, u32[]{:S(2)}) copy-start(bf16[1,512,128]{2,1,0:T(8,128)(2,1)} %param.6) | copy-start | bytes 393220
  440.6 5.7 %copy-start.16 = (f32[128]{0:T(128)S(1)}, f32[128]{0:T(128)}, u32[]{:S(2)}) copy-start(f32[128]{0:T(128)} %param.11) | copy-start | bytes 1540
Sparse Core Ops, SparseCore 0:
  242.0 73.7 all-reduce.2
where the time goes:
time: 491 us; the launch traced here: 486 us
  other arithmetic  160 us (33%)
  local copies, waits for them, and re-layouts  120 us (24%)
  waiting for transfers between devices  108 us (22%)
  starting transfers between devices  41.7 us (8%)
  matrix products  41.6 us (8%)
  between operations  14.9 us (3%)
    unnamed x3, other arithmetic  149 us
    psum x1, waiting for transfers between devices, channel_layout(): grad_time = lax.psum(jnp.transpose(joined[spread:], (1, 0)), 'dp')  77 us
    unnamed x49, local copies, waits for them, and re-layouts  51.3 us
    all_to_all x1, local copies, waits for them, and re-layouts, channel_layout(): lax.all_to_all(grad_time[None], 'seq', split_axis=1, concat_axis=2, tiled...  15 us
    psum x1, local copies, waits for them, and re-layouts, channel_layout(): grad_time = lax.psum(jnp.transpose(joined[spread:], (1, 0)), 'dp')  14.8 us
    all_to_all x1, starting transfers between devices, channel_layout(): lax.all_to_all(weighted, 'seq', split_axis=2, concat_axis=1, tiled=True)  14.2 us
    transpose x1, local copies, waits for them, and re-layouts, channel_layout(): jnp.transpose(joined[:spread].reshape(batch_local, narrow, length), (0, 2...  12 us
    all_to_all x1, waiting for transfers between devices, channel_layout(): lax.all_to_all(weighted, 'seq', split_axis=2, concat_axis=1, tiled=True)  11.4 us
  transfers between devices with their start and end apart: 6, of which 4 were waited for; matrix products, arithmetic and copies ran while one was open for 26% of the time, Pallas kernels for 0%

commit v1 on v0

--- a/solution.py
+++ b/solution.py
@@ -92,7 +92,7 @@
     back_imag = back_imag.reshape(2, -1, length)
     joined = (back_real[0] + back_real[1] * cos_twist - back_imag[1] * sin_twist) / (2.0 * length)
     convolved = jnp.transpose(joined[:spread].reshape(batch_local, narrow, length), (0, 2, 1))
-    grad_time = lax.psum(jnp.transpose(joined[spread:], (1, 0)), "dp")
+    grad_time = jnp.sum(lax.all_gather(jnp.transpose(joined[spread:], (1, 0)), "dp"), axis=0)
     convolved, grad_back = (
         lax.all_to_all(convolved, "seq", split_axis=1, concat_axis=2, tiled=True),
         lax.all_to_all(grad_time[None], "seq", split_axis=1, concat_axis=2, tiled=True),

time: 491 us -> 417 us (0.85)
  waiting for transfers between devices: 108 us -> 30.7 us
    psum x1 -> x0, waiting for transfers between devices: 77 us -> none  [channel_layout(): grad_time = lax.psum(jnp.transpose(joined[spread:], (1, 0)), 'dp')]
    psum x1 -> x0, local copies, waits for them, and re-layouts: 14.8 us -> none  [channel_layout(): grad_time = lax.psum(jnp.transpose(joined[spread:], (1, 0)), 'dp')]
    broadcast_in_dim x1, local copies, waits for them, and re-layouts: 0.78 us -> 12.1 us  [channel_layout(): grad_time[None]]
  transfers between devices with their start and end apart: 6 -> 6, of which waited for: 4 -> 3; matrix products, arithmetic and copies ran while one was open for 26% -> 54% of each run, Pallas kernels for 0% -> 0%
where the time goes in v1:
time: 417 us; the launch traced here: 412 us
  other arithmetic  163 us (39%)
  local copies, waits for them, and re-layouts  117 us (28%)
  starting transfers between devices  44.3 us (11%)
  matrix products  41.6 us (10%)
  waiting for transfers between devices  30.7 us (7%)
  between operations  14.9 us (4%)
    unnamed x3, other arithmetic  150 us
    unnamed x49, local copies, waits for them, and re-layouts  50.9 us
    all_to_all x1, local copies, waits for them, and re-layouts, channel_layout(): lax.all_to_all(grad_time[None], 'seq', split_axis=1, concat_axis=2, tiled...  15 us
    all_to_all x1, starting transfers between devices, channel_layout(): lax.all_to_all(weighted, 'seq', split_axis=2, concat_axis=1, tiled=True)  14.2 us
    all_to_all x1, starting transfers between devices, channel_layout(): lax.all_to_all(grad_time[None], 'seq', split_axis=1, concat_axis=2, tiled...  12.5 us
    transpose x1, local copies, waits for them, and re-layouts, channel_layout(): jnp.transpose(joined[:spread].reshape(batch_local, narrow, length), (0, 2...  12.1 us
    broadcast_in_dim x1, local copies, waits for them, and re-layouts, channel_layout(): grad_time[None]  12.1 us
    all_to_all x1, waiting for transfers between devices, channel_layout(): lax.all_to_all(weighted, 'seq', split_axis=2, concat_axis=1, tiled=True)  11.4 us
  transfers between devices with their start and end apart: 6, of which 3 were waited for; matrix products, arithmetic and copies ran while one was open for 54% of the time, Pallas kernels for 0%

profile of v1, /device:TPU:2, one launch (start us, length us, event | category | flops | bytes accessed | tf_op | source)
XLA Modules:
  0.0 411.7 jit_solution(8138178048912847619)
XLA Ops:
  7.2 1.1 convert_multiply_fusion.1
  8.3 0.8 copy.202
  9.1 14.2 %all-to-all-start.2 = ((f32[1,512,128]{1,0,2:T(1,128)}), f32[1,512,128]{1,0,2:T(1,128)S(1)}, u32[]{:S(2)}, u32[]{:S(2)}) async-start(f32[1,512,128]{1,0,2:T(1,128)} %copy.202), calls=%async_computation.2 | async-start | bytes 524288 | tf_op jit(solution)/shard_map/all_to_all | solution.py:59
  23.4 0.8 copy.256
  24.2 11.4 %all-to-all-done.2 = f32[1,512,128]{1,0,2:T(1,128)S(1)} async-done(((f32[1,512,128]{1,0,2:T(1,128)}), f32[1,512,128]{1,0,2:T(1,128)S(1)}, u32[]{:S(2)}, u32[]{:S(2)}) %all-to-all-start.2) | async-done | bytes 262176 | tf_op jit(solution)/shard_map/all_to_all | solution.py:59
  35.6 5.0 %all-to-all-start.1 = ((f32[1,512,128]{1,0,2:T(1,128)}), f32[1,512,128]{1,0,2:T(1,128)S(1)}, u32[]{:S(2)}, u32[]{:S(2)}) async-start(f32[1,512,128]{1,0,2:T(1,128)} %copy.256), calls=%async_computation.1 | async-start | bytes 524288 | tf_op jit(solution)/shard_map/all_to_all | solution.py:60
  40.6 0.8 copy.198
  41.4 0.3 fusion.72
  41.7 0.3 fusion.71
  42.0 0.3 broadcast_multiply_fusion.1
  42.2 10.6 %all-to-all-done.1 = f32[1,512,128]{1,0,2:T(1,128)S(1)} async-done(((f32[1,512,128]{1,0,2:T(1,128)}), f32[1,512,128]{1,0,2:T(1,128)S(1)}, u32[]{:S(2)}, u32[]{:S(2)}) %all-to-all-start.1) | async-done | bytes 262176 | tf_op jit(solution)/shard_map/all_to_all | solution.py:60
  52.9 5.8 %all-to-all-start = ((f32[1,512,128]{1,0,2:T(1,128)}), f32[1,512,128]{1,0,2:T(1,128)S(1)}, u32[]{:S(2)}, u32[]{:S(2)}) async-start(f32[1,512,128]{1,0,2:T(1,128)} %copy.198), calls=%async_computation | async-start | bytes 524288 | tf_op jit(solution)/shard_map/all_to_all | solution.py:58
  58.7 0.3 all-gather.3.cloned.1.call-start
  59.1 0.2 fusion.22
  59.4 0.7 copy.226
  60.6 0.9 fusion.50
  62.3 8.6 %all-to-all-done = f32[1,512,128]{1,0,2:T(1,128)S(1)} async-done(((f32[1,512,128]{1,0,2:T(1,128)}), f32[1,512,128]{1,0,2:T(1,128)S(1)}, u32[]{:S(2)}, u32[]{:S(2)}) %all-to-all-start) | async-done | bytes 262176 | tf_op jit(solution)/shard_map/all_to_all | solution.py:58
  71.8 0.3 copy.262
  72.1 1.7 fusion.7
  73.8 2.8 fusion.45
  76.6 2.8 convolution_subtract_fusion
  79.5 1.7 convolution_add_fusion
  81.1 3.4 fusion.11
  84.5 4.0 fusion.15
  88.5 4.0 add_bitcast_fusion
  92.5 3.0 copy.220
  95.6 3.1 reshape_reshape.15
  98.6 5.4 %subtract_bitcast_fusion = f32[24,128,128]{1,2,0:T(8,128)} fusion(f32[24,128,128]{2,1,0:T(8,128)} %fusion.15, f32[24,128,128]{2,1,0:T(8,128)S(1)} %convolution_add_fusion, f32[24,128,128]{2,1,0:T(8,128)S(1)} %convolution_subtract_fusion, f32[128,128]{0,1:T(8,128)S(1)} %copy.214, f32[128,128]{0,1:T(8,128)S(1)} %copy.212), kind=kOutput, calls=%fused_computation.9 | convolution fusion | flops 605798400 | bytes 6422528 | tf_op jit(solution)/shard_map/ckq,jq->ckj/dot_general | solution.py:44
  104.0 3.2 copy.217
  107.2 3.2 reshape_reshape.14
  110.4 2.4 multiply_subtract_fusion.2
  112.8 0.4 maximum_bitcast_fusion
  113.5 1.9 fusion.41
  115.6 1.9 fusion.39
  117.6 1.9 fusion.5
  119.5 1.9 fusion.4
  121.5 2.0 fusion.18
  123.5 2.2 fusion.17
  125.7 2.0 fusion.2
  127.7 0.8 slice.55
  128.5 2.0 copy.233
  130.6 2.0 fusion.3
  133.1 0.6 copy-done.5
  133.7 0.9 fusion.9
  134.7 0.8 slice_bitcast_fusion
  135.5 12.1 %copy.234 = f32[1,16384,4]{2,0,1:T(1,128)} copy(f32[1,16384,4]{1,2,0:T(4,128)S(1)} %get-tuple-element.19) | data formatting | bytes 524288 | tf_op jit(solution)/shard_map/transpose | solution.py:94
  147.6 0.6 broadcast.236
  148.2 74.5 %reduce = f32[16384,4]{1,0:T(8,128)} reduce(f32[16384,1,4]{2,1,0:T(1,128)} %bitcast.183, f32[]{:T(128)} %broadcast.236), dimensions={1}, to_apply=%bitcast.167.reduce_sub_computation | reduce | bytes 524292
  222.7 9.1 %reshape.144 = f32[32,1,2048]{2,1,0:T(1,128)} reshape(f32[16384,4]{1,0:T(8,128)} %reduce) | data formatting | bytes 524288
  231.8 6.4 %all-to-all-start.3 = ((f32[32,1,2048]{2,1,0:T(1,128)}), f32[32,1,2048]{2,1,0:T(1,128)S(1)}, u32[]{:S(2)}, u32[]{:S(2)}) async-start(f32[32,1,2048]{2,1,0:T(1,128)} %reshape.144), calls=%async_computation.3 | async-start | bytes 524288 | tf_op jit(solution)/shard_map/all_to_all | solution.py:97
  238.2 3.3 bitcast_reduce_fusion
  241.5 12.1 %copy.238 = f32[1,16384,4]{2,0,1:T(1,128)} copy(f32[1,16384,4]{1,2,0:T(4,128)S(1)} %bitcast.203) | data formatting | bytes 524288 | tf_op jit(solution)/shard_map/broadcast_in_dim | solution.py:98
  253.6 74.5 %reduce.2 = f32[16384,4]{1,0:T(8,128)} reduce(f32[16384,1,4]{2,1,0:T(1,128)} %bitcast.184, f32[]{:T(128)} %broadcast.236), dimensions={1}, to_apply=%bitcast.169.reduce_sub_computation | reduce | bytes 524292
  328.2 9.1 %reshape.146 = f32[32,1,2048]{2,1,0:T(1,128)} reshape(f32[16384,4]{1,0:T(8,128)} %reduce.2) | data formatting | bytes 524288
  337.2 12.5 %all-to-all-start.4 = ((f32[32,1,2048]{2,1,0:T(1,128)}), f32[32,1,2048]{2,1,0:T(1,128)S(1)}, u32[]{:S(2)}, u32[]{:S(2)}) async-start(f32[32,1,2048]{2,1,0:T(1,128)} %reshape.146), calls=%async_computation.4 | async-start | bytes 524288 | tf_op jit(solution)/shard_map/all_to_all | solution.py:98
  349.7 1.3 reduce.1
  351.0 14.8 %reshape.145 = f32[16384,1,4]{2,1,0:T(1,128)} reshape(f32[32,2048]{1,0:T(8,128)S(1)} %reduce.1) | data formatting | bytes 524288
  365.8 5.3 %copy.257 = f32[1,32,512,4]{2,1,3,0:T(8,128)S(1)} copy(f32[1,32,512,4]{3,2,1,0:T(8,128)} %bitcast.185) | data formatting | bytes 524288 | tf_op jit(solution)/shard_map/all_to_all | solution.py:97
  371.1 0.3 copy.236
  371.6 0.7 fusion.19
  372.3 1.3 reduce.3
  373.6 14.8 %reshape.147 = f32[16384,1,4]{2,1,0:T(1,128)} reshape(f32[32,2048]{1,0:T(8,128)S(1)} %reduce.3) | data formatting | bytes 524288
  388.4 15.0 %copy.239 = f32[1,16384,4]{1,2,0:T(4,128)S(1)} copy(f32[1,16384,4]{2,0,1:T(1,128)} %bitcast.186) | data formatting | bytes 524288 | tf_op jit(solution)/shard_map/all_to_all | solution.py:98
  403.8 0.8 copy.241
  (67 shorter events, 3.7 us)
Async XLA Ops:
  7.2 16.2 %copy-start.15 = (f32[512,128]{1,0:T(8,128)S(1)}, f32[512,128]{1,0:T(8,128)}, u32[]{:S(2)}) copy-start(f32[512,128]{1,0:T(8,128)} %param.10) | copy-start | bytes 786436
  7.2 33.4 %copy-start.10 = (bf16[1,512,128]{2,1,0:T(8,128)(2,1)S(1)}, bf16[1,512,128]{2,1,0:T(8,128)(2,1)}, u32[]{:S(2)}) copy-start(bf16[1,512,128]{2,1,0:T(8,128)(2,1)} %param.7) | copy-start | bytes 393220
  7.2 33.4 %copy-start.12 = (bf16[1,512,128]{2,1,0:T(8,128)(2,1)S(1)}, bf16[1,512,128]{2,1,0:T(8,128)(2,1)}, u32[]{:S(2)}) copy-start(bf16[1,512,128]{2,1,0:T(8,128)(2,1)} %param.6) | copy-start | bytes 393220
  9.1 26.5 %all-to-all-start.2 = ((f32[1,512,128]{1,0,2:T(1,128)}), f32[1,512,128]{1,0,2:T(1,128)S(1)}, u32[]{:S(2)}, u32[]{:S(2)}) async-start(f32[1,512,128]{1,0,2:T(1,128)} %copy.202), calls=%async_computation.2 | async-start | bytes 524288 | tf_op jit(solution)/shard_map/all_to_all | solution.py:59
  35.6 17.3 %all-to-all-start.1 = ((f32[1,512,128]{1,0,2:T(1,128)}), f32[1,512,128]{1,0,2:T(1,128)S(1)}, u32[]{:S(2)}, u32[]{:S(2)}) async-start(f32[1,512,128]{1,0,2:T(1,128)} %copy.256), calls=%async_computation.1 | async-start | bytes 524288 | tf_op jit(solution)/shard_map/all_to_all | solution.py:60
  52.9 18.1 %all-to-all-start = ((f32[1,512,128]{1,0,2:T(1,128)}), f32[1,512,128]{1,0,2:T(1,128)S(1)}, u32[]{:S(2)}, u32[]{:S(2)}) async-start(f32[1,512,128]{1,0,2:T(1,128)} %copy.198), calls=%async_computation | async-start | bytes 524288 | tf_op jit(solution)/shard_map/all_to_all | solution.py:58
  58.7 179.5 %all-gather.3.cloned.1.call-start = ((), (), s32[]{:S(2)}) async-start(), calls=%async_computation.5 | async-start | bytes 2359296 | tf_op jit(solution)/shard_map/all_gather | solution.py:95
  60.6 10.8 %copy-start.7 = (f32[16384]{0:T(1024)}, f32[16384]{0:T(1024)S(1)}, u32[]{:S(2)}) copy-start(f32[16384]{0:T(1024)S(1)} %fusion.51) | copy-start | bytes 196612
  62.3 9.8 %copy-start.1 = (f32[4,128,128]{1,2,0:T(8,128)}, f32[4,128,128]{1,2,0:T(8,128)S(1)}, u32[]{:S(2)}) copy-start(f32[4,128,128]{1,2,0:T(8,128)S(1)} %copy.209) | copy-start | bytes 786436
  71.4 0.7 copy-start.3
  76.6 2.9 copy-start.2
  76.6 2.9 copy-start.4
  107.2 3.2 copy-start
  119.5 1.9 copy-start.6
  132.7 1.0 copy-start.5
  132.7 1.0 copy-start.8
  132.7 1.0 copy-start.14
  231.8 105.5 %all-to-all-start.3 = ((f32[32,1,2048]{2,1,0:T(1,128)}), f32[32,1,2048]{2,1,0:T(1,128)S(1)}, u32[]{:S(2)}, u32[]{:S(2)}) async-start(f32[32,1,2048]{2,1,0:T(1,128)} %reshape.144), calls=%async_computation.3 | async-start | bytes 524288 | tf_op jit(solution)/shard_map/all_to_all | solution.py:97
  337.2 35.1 %all-to-all-start.4 = ((f32[32,1,2048]{2,1,0:T(1,128)}), f32[32,1,2048]{2,1,0:T(1,128)S(1)}, u32[]{:S(2)}, u32[]{:S(2)}) async-start(f32[32,1,2048]{2,1,0:T(1,128)} %reshape.146), calls=%async_computation.4 | async-start | bytes 524288 | tf_op jit(solution)/shard_map/all_to_all | solution.py:98
  365.8 5.7 %copy-start.9 = (bf16[1,512,128]{2,1,0:T(8,128)(2,1)S(1)}, bf16[1,512,128]{2,1,0:T(8,128)(2,1)}, u32[]{:S(2)}) copy-start(bf16[1,512,128]{2,1,0:T(8,128)(2,1)} %param.8) | copy-start | bytes 393220
  365.8 5.7 %copy-start.11 = (bf16[1,512,128]{2,1,0:T(8,128)(2,1)S(1)}, bf16[1,512,128]{2,1,0:T(8,128)(2,1)}, u32[]{:S(2)}) copy-start(bf16[1,512,128]{2,1,0:T(8,128)(2,1)} %param.7) | copy-start | bytes 393220
  365.8 5.7 %copy-start.13 = (bf16[1,512,128]{2,1,0:T(8,128)(2,1)S(1)}, bf16[1,512,128]{2,1,0:T(8,128)(2,1)}, u32[]{:S(2)}) copy-start(bf16[1,512,128]{2,1,0:T(8,128)(2,1)} %param.6) | copy-start | bytes 393220
  365.8 5.7 %copy-start.16 = (f32[128]{0:T(128)S(1)}, f32[128]{0:T(128)}, u32[]{:S(2)}) copy-start(f32[128]{0:T(128)} %param.11) | copy-start | bytes 1540
Sparse Core Ops, SparseCore 0:
  135.6 36.9 all-gather.2
